TPU v7x, 32 devices: a whole 2x2x4 slice. The times are simulated.
32 devices in a mesh: row: 8 (over z, y), col: 4 (over x, core).
Axes of the slice: x: 2, y: 2, z: 4, core: 2. Of those that a mesh axis runs over, the one named last changes fastest.
Arguments:
- operator: bfloat16 [20480, 20480], P('row', 'col'), may hold values from -0.0625 to 0.0625
- panels: float32 [20480, 512], P(('row', 'col')), may hold values from -6 to 6
Outputs:
- adjoint: float32 [3, 20480, 512], P(None, ('row', 'col'))
All inputs are finite; a program needn't handle non-finite values.
Results may differ from a plain program's by a relative error of at most 0.0043.
Values may be sent and summed in bfloat16 or wider, within the bound.
A program may use at most 128 MiB of HBM per device.

v0:
```python
import functools

import jax
import jax.numpy as jnp
from jax import lax
from jax.experimental import pallas as pl
from jax.experimental.pallas import tpu as pltpu
from jax.sharding import PartitionSpec as P

APPS = 3
CHUNKS = 4
MESH = pl.DeviceIdType.MESH


def kernel(cols, panels_ref, op_ref, out_ref, x, own, opbuf, ysend, yrecv, fsend, bsend,
           brecv, frecv, op_sem, ys_sem, yr_sem, bs_sem, br_sem, fs_sem, fr_sem,
           xs_sem, xr_sem, x0s_sem, x0r_sem, os_sem, or_sem):
    zs = cols
    steps = CHUNKS * cols
    width = own.shape[2]
    row, col = lax.axis_index("row"), lax.axis_index("col")
    z, y = row // 2, row % 2
    root = z == col
    partner = (z * 2 + 1 - y, col)
    far = z // 2 != col // 2
    mate = jnp.logical_not(far) & (z != col)
    from_far = ((z >= col) & (z < zs - 1) & ((z + 1) // 2 != col // 2)) | (
        (z <= col) & (z > 0) & ((z - 1) // 2 != col // 2)
    )
    across = lax.rem(z + cols // 2, cols)
    relay = col == across
    sibling = col + 1 - 2 * (col % 2)
    onward = (jnp.where(z > col, row - 2, row + 2), col)
    others = [lax.rem(col + d, cols) for d in range(1, cols)]

    barrier = pltpu.get_barrier_semaphore()
    pl.semaphore_signal(barrier, inc=1, device_id=partner, device_id_type=MESH)
    for other in others:
        pl.semaphore_signal(barrier, inc=1, device_id=(row, other), device_id_type=MESH)

    @pl.when(z > 0)
    def _():
        pl.semaphore_signal(barrier, inc=1, device_id=(row - 2, col), device_id_type=MESH)

    @pl.when(z < zs - 1)
    def _():
        pl.semaphore_signal(barrier, inc=1, device_id=(row + 2, col), device_id_type=MESH)

    def op_copy(slot, step):
        half = 1 - y if slot == 0 else y
        first = pl.multiple_of((half * cols + step % cols) * width, 128)
        return pltpu.make_async_copy(
            op_ref.at[:, pl.ds(first, width)], opbuf.at[slot], op_sem.at[slot]
        )

    op_copy(0, 0).start()
    op_copy(1, 0).start()
    pl.semaphore_wait(
        barrier, cols + jnp.where(z > 0, 1, 0) + jnp.where(z < zs - 1, 1, 0)
    )

    def first_x(h, d, source):
        return pltpu.make_async_remote_copy(
            src_ref=panels_ref.at[h],
            dst_ref=x.at[0, h, source],
            send_sem=x0s_sem.at[h, d],
            recv_sem=x0r_sem.at[h, source],
            device_id=(row, others[d]),
            device_id_type=MESH,
        )

    for h in range(CHUNKS):
        for d in range(cols - 1):
            first_x(h, d, col).start()
        x[0, h, col] = panels_ref[h]

    def y_copy(app, step):
        return pltpu.make_async_remote_copy(
            src_ref=ysend.at[step],
            dst_ref=yrecv.at[app, step],
            send_sem=ys_sem.at[step],
            recv_sem=yr_sem.at[app, step],
            device_id=partner,
            device_id_type=MESH,
        )

    def bz_copy(app, step):
        return pltpu.make_async_remote_copy(
            src_ref=bsend.at[step],
            dst_ref=brecv.at[app, step],
            send_sem=bs_sem.at[step],
            recv_sem=br_sem.at[app, step],
            device_id=onward,
            device_id_type=MESH,
        )

    def fz_copy(app, step):
        return pltpu.make_async_remote_copy(
            src_ref=fsend.at[step],
            dst_ref=frecv.at[app, step],
            send_sem=fs_sem.at[step],
            recv_sem=fr_sem.at[app, step],
            device_id=onward,
            device_id_type=MESH,
        )

    def x_copy(app, step, d):
        block = x.at[app + 1, step // cols, step % cols]
        return pltpu.make_async_remote_copy(
            src_ref=block,
            dst_ref=block,
            send_sem=xs_sem.at[app, d, step],
            recv_sem=xr_sem.at[app, step],
            device_id=(row, sibling if d == 0 else across),
            device_id_type=MESH,
        )

    def out_local(app, step):
        return pltpu.make_async_copy(
            fsend.at[step], out_ref.at[app, step // cols], os_sem.at[app, step]
        )

    def out_copy(app, step):
        return pltpu.make_async_remote_copy(
            src_ref=fsend.at[step],
            dst_ref=out_ref.at[app, step // cols],
            send_sem=os_sem.at[app, step],
            recv_sem=or_sem.at[app, step // cols],
            device_id=(row, step % cols),
            device_id_type=MESH,
        )

    def out_wait(app, step):
        @pl.when(step % cols == col)
        def _():
            out_local(app, step).wait()

        @pl.when(step % cols != col)
        def _():
            out_copy(app, step).wait_send()

    def product(app, h, slot):
        total = None
        for k in range(cols):
            term = jnp.dot(
                x[app, h, k],
                opbuf[slot, k * width : (k + 1) * width, :],
                preferred_element_type=jnp.float32,
            )
            total = term if total is None else total + term
        return total

    for app in range(APPS):
        last = app == APPS - 1

        def next_op(slot, step, last=last):
            if last:
                @pl.when(step < steps - 1)
                def _():
                    op_copy(slot, step + 1).start()
            else:
                op_copy(slot, step + 1).start()

        def combine(step, carry, app=app, last=last):
            h, s = step // cols, step % cols
            acc = own.at[step % 2]
            y_copy(app, step).wait_recv()
            acc[...] += yrecv[app, step].astype(jnp.float32)

            @pl.when(from_far)
            def _():
                bz_copy(app, step).wait_recv()
                acc[...] += brecv[app, step].astype(jnp.float32)

            @pl.when(far)
            def _():
                if app > 0:
                    bz_copy(app - 1, step).wait_send()
                bsend[step] = acc[...].astype(jnp.bfloat16)
                bz_copy(app, step).start()

            @pl.when(mate)
            def _():
                if app > 0:
                    fz_copy(app - 1, step).wait_send()
                fsend[step] = acc[...]
                fz_copy(app, step).start()

            @pl.when(root)
            def _():
                fz_copy(app, step).wait_recv()
                acc[...] += frecv[app, step]
                if not last:
                    x[app + 1, h, s] = acc[...].astype(jnp.bfloat16)
                    x_copy(app, step, 1).start()
                    x_copy(app, step, 0).start()
                if app > 0:
                    out_wait(app - 1, step)
                fsend[step] = acc[...]

                @pl.when(s == col)
                def _():
                    out_local(app, step).start()

                @pl.when(s != col)
                def _():
                    out_copy(app, step).start()

            return carry

        def one(step, carry, app=app):
            h, s = step // cols, step % cols

            @pl.when(s == 0)
            def _():
                if app == 0:
                    for d in range(cols - 1):
                        first_x(h, d, others[d]).wait_recv()
                else:
                    @pl.when(jnp.logical_not(root))
                    def _():
                        for k in range(cols):
                            x_copy(app - 1, h * cols + k, 0).wait_recv()

                            @pl.when(relay)
                            def _():
                                x_copy(app - 1, h * cols + k, 0).start()

            op_copy(0, step).wait()
            theirs = product(app, h, 0)
            next_op(0, step)
            if app > 0:
                y_copy(app - 1, step).wait_send()
            ysend[step] = theirs.astype(jnp.bfloat16)
            y_copy(app, step).start()
            op_copy(1, step).wait()
            own[step % 2] = product(app, h, 1)
            next_op(1, step)
            lax.fori_loop(
                jnp.where(s > 0, step - 1, step),
                jnp.where(s == cols - 1, step + 1, step),
                combine,
                0,
            )
            return carry

        lax.fori_loop(0, steps, one, 0)

    def finish(step, carry):
        y_copy(APPS - 1, step).wait_send()

        @pl.when(root)
        def _():
            out_wait(APPS - 1, step)
            for app in range(APPS - 1):
                x_copy(app, step, 0).wait_send()
                x_copy(app, step, 1).wait_send()

        @pl.when(relay)
        def _():
            for app in range(APPS - 1):
                x_copy(app, step, 0).wait_send()

        @pl.when(far)
        def _():
            bz_copy(APPS - 1, step).wait_send()

        @pl.when(mate)
        def _():
            fz_copy(APPS - 1, step).wait_send()

        return carry

    lax.fori_loop(0, steps, finish, 0)
    for h in range(CHUNKS):
        for d in range(cols - 1):
            first_x(h, d, col).wait_send()

    @pl.when(jnp.logical_not(root))
    def _():
        for app in range(APPS):
            for h in range(CHUNKS):
                out_copy(app, h * cols + col).wait_recv()


def by_kernel(operator, panels):
    cols = lax.axis_size("col")
    width, count = panels.shape
    part = count // CHUNKS
    steps = CHUNKS * cols
    turned = panels.astype(jnp.bfloat16).T.reshape(CHUNKS, part, width)
    block = (part, width)
    dma = pltpu.SemaphoreType.DMA
    out = pl.pallas_call(
        functools.partial(kernel, cols),
        out_shape=jax.ShapeDtypeStruct((APPS, CHUNKS) + block, jnp.float32),
        in_specs=[
            pl.BlockSpec(memory_space=pltpu.VMEM),
            pl.BlockSpec(memory_space=pl.ANY),
        ],
        out_specs=pl.BlockSpec(memory_space=pl.ANY),
        scratch_shapes=[
            pltpu.VMEM((APPS, CHUNKS, cols) + block, jnp.bfloat16),
            pltpu.VMEM((2,) + block, jnp.float32),
            pltpu.VMEM((2, operator.shape[0], width), jnp.bfloat16),
            pltpu.VMEM((steps,) + block, jnp.bfloat16),
            pltpu.VMEM((APPS, steps) + block, jnp.bfloat16),
            pltpu.VMEM((steps,) + block, jnp.float32),
            pltpu.VMEM((steps,) + block, jnp.bfloat16),
            pltpu.VMEM((APPS, steps) + block, jnp.bfloat16),
            pltpu.VMEM((APPS, steps) + block, jnp.float32),
            dma((2,)),
            dma((steps,)),
            dma((APPS, steps)),
            dma((steps,)),
            dma((APPS, steps)),
            dma((steps,)),
            dma((APPS, steps)),
            dma((APPS - 1, 2, steps)),
            dma((APPS - 1, steps)),
            dma((CHUNKS, cols - 1)),
            dma((CHUNKS, cols)),
            dma((APPS, steps)),
            dma((APPS, CHUNKS)),
        ],
        compiler_params=pltpu.CompilerParams(
            collective_id=0, has_side_effects=True, vmem_limit_bytes=62 * 2**20
        ),
        cost_estimate=pl.CostEstimate(
            flops=APPS * 2 * operator.size * count,
            bytes_accessed=APPS * CHUNKS * operator.size * 2,
            transcendentals=0,
        ),
    )(turned, operator)
    return out.reshape(APPS, count, width).transpose(0, 2, 1)


def by_collectives(operator, panels):
    rows = lax.axis_size("row")
    cols = lax.axis_size("col")
    perm = [(r * cols + c, c * rows + r) for r in range(rows) for c in range(cols)]
    results = []
    current = panels
    for repeat in range(APPS):
        rounded = current.astype(jnp.bfloat16)
        gathered = lax.all_gather(rounded, "col", axis=0, tiled=True)
        partial = lax.dot_general(
            operator,
            gathered,
            (((0,), (0,)), ((), ())),
            preferred_element_type=jnp.float32,
        )
        mine = lax.psum_scatter(partial, "row", scatter_dimension=0, tiled=True)
        current = lax.ppermute(mine, ("row", "col"), perm)
        results.append(current)
    return jnp.stack(results)


def solution(mesh):
    fits = mesh.shape["row"] == 8 and mesh.shape["col"] == 4
    in_specs = (P("row", "col"), P(("row", "col"), None))
    out_specs = P(None, ("row", "col"), None)
    return jax.shard_map(
        by_kernel if fits else by_collectives,
        mesh=mesh,
        in_specs=in_specs,
        out_specs=out_specs,
        check_vma=False,
    )
```

profile of v0, /device:TPU:0, one launch (start us, length us, event | category | flops | bytes accessed | tf_op | source)
XLA Modules:
  0.0 249.1 jit_solution(10081931674395091474)
XLA Ops:
  0.0 1.4 convert_bitcast_fusion
  1.4 1.1 copy.3
  2.5 241.2 %shard_map.28 = f32[3,4,128,640]{3,2,1,0:T(8,128)} custom-call(bf16[4,128,640]{2,1,0:T(8,128)(2,1)} %bitcast.6, bf16[2560,5120]{1,0:T(8,128)(2,1)} %op_ref.1), custom_call_target="tpu_custom_call" | custom-call | flops 40265318400 | bytes 314572800 | tf_op jit(solution)/shard_map/pallas_call | solution.py:294
  243.6 5.5 %copy.4 = f32[3,512,640]{1,2,0:T(8,128)} copy(f32[3,512,640]{2,1,0:T(8,128)} %bitcast.5) | data formatting | bytes 7864320 | tf_op jit(solution)/shard_map/reshape | solution.py:335
where the time goes:
time: 250 us; the launch traced here: 249 us
  Pallas kernels  241 us (96%)
  local copies, waits for them, and re-layouts  6.53 us (3%)
    pallas_call x1, Pallas kernels, by_kernel(): pl.pallas_call(functools.partial(kernel, cols), out_shape=jax.ShapeDtypeS...  241 us
    reshape x1, local copies, waits for them, and re-layouts, by_kernel(): return out.reshape(APPS, count, width).transpose(0, 2, 1)  5.45 us

commit v1 on v0

--- a/solution.py
+++ b/solution.py
@@ -9,6 +9,8 @@
 
 APPS = 3
 CHUNKS = 4
+LAG = 1
+RELAY = 9
 MESH = pl.DeviceIdType.MESH
 
 
@@ -150,101 +152,121 @@
             total = term if total is None else total + term
         return total
 
-    for app in range(APPS):
-        last = app == APPS - 1
-
-        def next_op(slot, step, last=last):
-            if last:
-                @pl.when(step < steps - 1)
-                def _():
-                    op_copy(slot, step + 1).start()
-            else:
-                op_copy(slot, step + 1).start()
-
-        def combine(step, carry, app=app, last=last):
-            h, s = step // cols, step % cols
-            acc = own.at[step % 2]
-            y_copy(app, step).wait_recv()
-            acc[...] += yrecv[app, step].astype(jnp.float32)
-
-            @pl.when(from_far)
-            def _():
-                bz_copy(app, step).wait_recv()
-                acc[...] += brecv[app, step].astype(jnp.float32)
-
-            @pl.when(far)
-            def _():
-                if app > 0:
-                    bz_copy(app - 1, step).wait_send()
-                bsend[step] = acc[...].astype(jnp.bfloat16)
-                bz_copy(app, step).start()
-
-            @pl.when(mate)
-            def _():
-                if app > 0:
-                    fz_copy(app - 1, step).wait_send()
-                fsend[step] = acc[...]
-                fz_copy(app, step).start()
-
-            @pl.when(root)
-            def _():
-                fz_copy(app, step).wait_recv()
-                acc[...] += frecv[app, step]
-                if not last:
-                    x[app + 1, h, s] = acc[...].astype(jnp.bfloat16)
-                    x_copy(app, step, 1).start()
-                    x_copy(app, step, 0).start()
-                if app > 0:
-                    out_wait(app - 1, step)
-                fsend[step] = acc[...]
-
-                @pl.when(s == col)
-                def _():
-                    out_local(app, step).start()
-
-                @pl.when(s != col)
-                def _():
-                    out_copy(app, step).start()
-
-            return carry
-
-        def one(step, carry, app=app):
-            h, s = step // cols, step % cols
-
-            @pl.when(s == 0)
-            def _():
-                if app == 0:
-                    for d in range(cols - 1):
-                        first_x(h, d, others[d]).wait_recv()
-                else:
-                    @pl.when(jnp.logical_not(root))
-                    def _():
-                        for k in range(cols):
-                            x_copy(app - 1, h * cols + k, 0).wait_recv()
-
-                            @pl.when(relay)
-                            def _():
-                                x_copy(app - 1, h * cols + k, 0).start()
-
-            op_copy(0, step).wait()
-            theirs = product(app, h, 0)
-            next_op(0, step)
-            if app > 0:
-                y_copy(app - 1, step).wait_send()
-            ysend[step] = theirs.astype(jnp.bfloat16)
-            y_copy(app, step).start()
-            op_copy(1, step).wait()
-            own[step % 2] = product(app, h, 1)
-            next_op(1, step)
-            lax.fori_loop(
-                jnp.where(s > 0, step - 1, step),
-                jnp.where(s == cols - 1, step + 1, step),
-                combine,
-                0,
-            )
-            return carry
-
-        lax.fori_loop(0, steps, one, 0)
+    total = APPS * steps
+
+    def make(turn):
+        app, step = turn // steps, turn % steps
+        h, s = step // cols, step % cols
+
+        @pl.when((s == 0) & (app == 0))
+        def _():
+            for d in range(cols - 1):
+                first_x(h, d, others[d]).wait_recv()
+
+        @pl.when((s == 0) & (app > 0) & jnp.logical_not(root) & jnp.logical_not(relay))
+        def _():
+            for k in range(cols):
+                x_copy(app - 1, h * cols + k, 0).wait_recv()
+
+        op_copy(0, step).wait()
+        theirs = product(app, h, 0)
+
+        @pl.when(turn < total - 1)
+        def _():
+            op_copy(0, step + 1).start()
+
+        @pl.when(app > 0)
+        def _():
+            y_copy(app - 1, step).wait_send()
+
+        ysend[step] = theirs.astype(jnp.bfloat16)
+        y_copy(app, step).start()
+        op_copy(1, step).wait()
+        own[turn % (LAG + 1)] = product(app, h, 1)
+
+        @pl.when(turn < total - 1)
+        def _():
+            op_copy(1, step + 1).start()
+
+    def combine(turn):
+        app, step = turn // steps, turn % steps
+        h, s = step // cols, step % cols
+        acc = own.at[turn % (LAG + 1)]
+        y_copy(app, step).wait_recv()
+        acc[...] += yrecv[app, step].astype(jnp.float32)
+
+        @pl.when(from_far)
+        def _():
+            bz_copy(app, step).wait_recv()
+            acc[...] += brecv[app, step].astype(jnp.float32)
+
+        @pl.when(far)
+        def _():
+            @pl.when(app > 0)
+            def _():
+                bz_copy(app - 1, step).wait_send()
+
+            bsend[step] = acc[...].astype(jnp.bfloat16)
+            bz_copy(app, step).start()
+
+        @pl.when(mate)
+        def _():
+            @pl.when(app > 0)
+            def _():
+                fz_copy(app - 1, step).wait_send()
+
+            fsend[step] = acc[...]
+            fz_copy(app, step).start()
+
+        @pl.when(root)
+        def _():
+            fz_copy(app, step).wait_recv()
+            acc[...] += frecv[app, step]
+
+            @pl.when(app < APPS - 1)
+            def _():
+                x[app + 1, h, s] = acc[...].astype(jnp.bfloat16)
+                x_copy(app, step, 1).start()
+                x_copy(app, step, 0).start()
+
+            @pl.when(app > 0)
+            def _():
+                out_wait(app - 1, step)
+
+            fsend[step] = acc[...]
+
+            @pl.when(s == col)
+            def _():
+                out_local(app, step).start()
+
+            @pl.when(s != col)
+            def _():
+                out_copy(app, step).start()
+
+    def forward(turn):
+        app, step = turn // steps, turn % steps
+
+        @pl.when(relay)
+        def _():
+            x_copy(app, step, 0).wait_recv()
+            x_copy(app, step, 0).start()
+
+    def one(turn, carry):
+        @pl.when((turn >= LAG + RELAY) & (turn < LAG + RELAY + total - steps))
+        def _():
+            forward(turn - LAG - RELAY)
+
+        @pl.when(turn < total)
+        def _():
+            make(turn)
+
+        @pl.when(turn >= LAG)
+        def _():
+            combine(turn - LAG)
+
+        return carry
+
+    lax.fori_loop(0, total + LAG, one, 0)
 
     def finish(step, carry):
         y_copy(APPS - 1, step).wait_send()
@@ -301,7 +323,7 @@
         out_specs=pl.BlockSpec(memory_space=pl.ANY),
         scratch_shapes=[
             pltpu.VMEM((APPS, CHUNKS, cols) + block, jnp.bfloat16),
-            pltpu.VMEM((2,) + block, jnp.float32),
+            pltpu.VMEM((LAG + 1,) + block, jnp.float32),
             pltpu.VMEM((2, operator.shape[0], width), jnp.bfloat16),
             pltpu.VMEM((steps,) + block, jnp.bfloat16),
             pltpu.VMEM((APPS, steps) + block, jnp.bfloat16),

time: 250 us -> 218 us (0.87)
  Pallas kernels: 241 us -> 209 us
    pallas_call x1, Pallas kernels: 241 us -> 209 us  [by_kernel(): pl.pallas_call(functools.partial(kernel, cols), out_shape=jax.ShapeDtypeS...]
where the time goes in v1:
time: 218 us; the launch traced here: 217 us
  Pallas kernels  209 us (96%)
  local copies, waits for them, and re-layouts  6.53 us (3%)
    pallas_call x1, Pallas kernels, by_kernel(): pl.pallas_call(functools.partial(kernel, cols), out_shape=jax.ShapeDtypeS...  209 us
    reshape x1, local copies, waits for them, and re-layouts, by_kernel(): return out.reshape(APPS, count, width).transpose(0, 2, 1)  5.45 us

profile of v1, /device:TPU:0, one launch (start us, length us, event | category | flops | bytes accessed | tf_op | source)
XLA Modules:
  0.0 217.1 jit_solution(15322238230675060057)
XLA Ops:
  0.0 1.4 convert_bitcast_fusion
  1.4 1.1 copy.3
  2.5 209.2 %shard_map.28 = f32[3,4,128,640]{3,2,1,0:T(8,128)} custom-call(bf16[4,128,640]{2,1,0:T(8,128)(2,1)} %bitcast.6, bf16[2560,5120]{1,0:T(8,128)(2,1)} %op_ref.1), custom_call_target="tpu_custom_call" | custom-call | flops 40265318400 | bytes 314572800 | tf_op jit(solution)/shard_map/pallas_call | solution.py:316
  211.6 5.5 %copy.4 = f32[3,512,640]{1,2,0:T(8,128)} copy(f32[3,512,640]{2,1,0:T(8,128)} %bitcast.5) | data formatting | bytes 7864320 | tf_op jit(solution)/shard_map/reshape | solution.py:357
